TPU v7x, 32 devices: a whole 2x2x4 slice. The times are simulated.
32 devices in a mesh: firm: 8 (over y, x, core), day: 4 (over z).
Axes of the slice: x: 2, y: 2, z: 4, core: 2. Of those that a mesh axis runs over, the one named last changes fastest.
Arguments:
- panel: float32 [65, 32, 4096], P(None, 'day', 'firm'), may hold values from -60 to 60, as said below
- presence: int32 [32, 4096], P(None, 'firm'), may hold values from 0 to 1, as said below
- firm_count: int32 [4096], P('firm'), may hold values from 1 to 32, as said below
- day_count: int32 [32], replicated, may hold values from 128 to 4096, as said below
Outputs:
- coefficients: float32 [64], replicated
- residual_panel: float32 [32, 4096], P('day', 'firm')
Inputs may be any that keep to these rules, and one draw needn't show every extreme that they name: presence is 0 or 1; every firm has at least one entry and every day at least 128 entries; some firm is present on every day and some day holds every firm; presence rates differ strongly across firms and days. firm_count is the number of ones of presence in that firm's column. day_count is the number of ones of presence in that day's row. `panel`: values at absent entries are arbitrary and are not used.
All inputs are finite; a program needn't handle non-finite values.
Results may differ from a plain program's by a relative error of at most 0.00025.
Values sent between devices are 32-bit elements; how exact they have to be, the bound alone decides.
A program may use at most 64 MiB of HBM per device.

v0:
```python
import jax
import jax.numpy as jnp
from jax import lax
from jax.sharding import PartitionSpec as P

K = 64
SWEEPS = 3


def cross_products(block):
    flat = block.reshape(block.shape[0], -1)
    return jnp.dot(flat, flat.T, precision=lax.Precision.HIGHEST)


def firm_totals(current):
    return lax.psum(jnp.sum(current, axis=1), "day")


def axis_day_sum(day_part):
    return lax.psum(day_part, "firm")


def axis_day_gram(day_part, gram_part):
    return lax.psum((day_part, gram_part), "firm")


def on_device(panel, presence, firm_count, day_count):
    cols, day_dev, firm_dev = panel.shape
    start = lax.axis_index("day") * day_dev
    mask_all = presence.astype(jnp.float32)
    mask_here = lax.dynamic_slice_in_dim(mask_all, start, day_dev, 0)
    firm_n = firm_count.astype(jnp.float32)
    day_all_n = day_count.astype(jnp.float32)
    day_here_n = lax.dynamic_slice_in_dim(day_all_n, start, day_dev, 0)
    current = panel * mask_here[None]
    gram = None
    for sweep in range(SWEEPS):
        last = sweep == SWEEPS - 1
        firm_mean = firm_totals(current) / firm_n
        demeaned = mask_here[None] * (current - firm_mean[:, None, :])
        day_part = jnp.sum(demeaned, axis=2)
        if last:
            totals, gram_total = axis_day_gram(day_part, cross_products(demeaned))
            day_mean = totals / day_here_n
            weighted = day_mean * day_here_n
            local_gram = gram_total - jnp.dot(weighted, day_mean.T, precision=lax.Precision.HIGHEST)
            gram = lax.psum(local_gram, "day")
        else:
            day_mean = axis_day_sum(day_part) / day_here_n
        current = mask_here[None] * (demeaned - day_mean[:, :, None])
    matrix = gram[:K, :K]
    target = gram[:K, K:]
    factor = jnp.linalg.cholesky(matrix)
    middle = lax.linalg.triangular_solve(factor, target, left_side=True, lower=True)
    coefficients = lax.linalg.triangular_solve(
        factor, middle, left_side=True, lower=True, transpose_a=True
    )[:, 0]
    fitted = jnp.tensordot(coefficients, current[:K], axes=1, precision=lax.Precision.HIGHEST)
    residual_panel = mask_here * (current[K] - fitted)
    return (coefficients, residual_panel)


def solution(mesh):
    placed = (P(None, "day", "firm"), P(None, "firm"), P("firm"), P())
    return jax.shard_map(
        on_device, mesh=mesh, in_specs=placed, out_specs=(P(), P("day", "firm")), check_vma=False
    )
```

profile of v0, /device:TPU:0, one launch (start us, length us, event | category | flops | bytes accessed | tf_op | source)
XLA Modules:
  0.0 232.9 jit_solution(7943531672309159769)
XLA Ops:
  7.2 0.0 copy-start
  7.2 0.0 copy-start.2
  7.2 0.0 copy-start.3
  7.2 0.0 all-reduce.5.cloned.1.call-start
  7.2 0.8 dynamic-slice_convert_fusion
  8.0 2.2 multiply_reduce_fusion
  10.3 0.0 all-reduce.5.cloned.1.call-update
  10.3 0.0 all-reduce.7.cloned.1.call-start
  10.3 0.0 copy-done.2
  10.4 0.0 copy-done.3
  10.4 0.1 dynamic_slice.7
  10.5 37.0 %all-reduce.5.cloned.1.call-done = f32[65,512]{1,0:T(8,128)} async-done(((f32[65,512]{1,0:T(8,128)}), f32[65,512]{1,0:T(8,128)}) %all-reduce.5.cloned.1.call-update) | async-done | bytes 133136 | tf_op jit(solution)/shard_map/psum | solution.py:16
  47.5 0.9 broadcast_divide_fusion.2
  48.4 0.0 copy-done
  48.4 0.2 fusion.9
  48.7 22.7 %psum.57 = f32[65,8]{1,0:T(8,128)S(1)} all-reduce(f32[65,8]{1,0:T(8,128)S(1)} %fusion.9), channel_id=1, replica_groups=mesh['firm'=8,'day'=4] {'firm'}, use_global_device_ids=true, to_apply=%region_3.0 | all-reduce | flops 520 | bytes 4160 | tf_op jit(solution)/shard_map/psum | solution.py:20
  71.3 1.1 fusion.7
  72.5 0.0 all-reduce.7.cloned.1.call-update
  72.5 0.0 all-reduce.9.cloned.1.call-start
  72.6 33.6 %all-reduce.7.cloned.1.call-done = f32[65,512]{1,0:T(8,128)} async-done(((f32[65,512]{1,0:T(8,128)}), f32[65,512]{1,0:T(8,128)}) %all-reduce.7.cloned.1.call-update) | async-done | bytes 133136 | tf_op jit(solution)/shard_map/psum | solution.py:16
  106.1 0.9 broadcast_divide_fusion.1
  107.1 0.4 fusion.21
  107.5 22.7 %psum.59 = f32[65,8]{1,0:T(8,128)S(1)} all-reduce(f32[65,8]{1,0:T(8,128)S(1)} %fusion.21), channel_id=1, replica_groups=mesh['firm'=8,'day'=4] {'firm'}, use_global_device_ids=true, to_apply=%region_7.0 | all-reduce | flops 520 | bytes 4160 | tf_op jit(solution)/shard_map/psum | solution.py:20
  130.2 1.3 fusion.8
  131.5 0.0 all-reduce.9.cloned.1.call-update
  131.5 33.6 %all-reduce.9.cloned.1.call-done = f32[65,512]{1,0:T(8,128)} async-done(((f32[65,512]{1,0:T(8,128)}), f32[65,512]{1,0:T(8,128)}) %all-reduce.9.cloned.1.call-update) | async-done | bytes 133136 | tf_op jit(solution)/shard_map/psum | solution.py:16
  165.1 0.9 broadcast_divide_fusion
  166.1 0.6 fusion.22
  166.7 2.2 fusion.2
  168.9 23.2 %all-reduce = (f32[65,65]{0,1:T(8,128)S(1)}, f32[65,8]{1,0:T(8,128)S(1)}) all-reduce(f32[65,65]{0,1:T(8,128)S(1)} %fusion.2, f32[65,8]{1,0:T(8,128)S(1)} %get-tuple-element.4), channel_id=1, replica_groups=mesh['firm'=8,'day'=4] {'firm'}, use_global_device_ids=true, to_apply=%region_10.0 | all-reduce | flops 4745 | bytes 37960 | tf_op jit(solution)/shard_map/psum | solution.py:24
  192.1 0.2 convolution_subtract_fusion
  192.3 18.5 %psum.63 = f32[65,65]{0,1:T(8,128)S(1)} all-reduce(f32[65,65]{0,1:T(8,128)S(1)} %convolution_subtract_fusion), channel_id=1, replica_groups=mesh['firm'=8,'day'=4] {'day'}, use_global_device_ids=true, to_apply=%region_13.0 | all-reduce | flops 4225 | bytes 33800 | tf_op jit(solution)/shard_map/psum | solution.py:47
  210.8 0.1 copy.10
  210.9 5.8 %cholesky.16 = f32[64,64]{1,0:T(8,128)S(1)} custom-call(f32[64,64]{1,0:T(8,128)S(1)} %fusion.15), custom_call_target="Cholesky" | custom-call | tf_op jit(solution)/shard_map/jit(cholesky)/cholesky | solution.py:53
  216.8 0.6 compare_reduce_fusion
  217.4 0.7 fusion.11
  218.1 4.9 %custom-call.8 = f32[1,64,64]{1,2,0:T(8,128)S(1)} custom-call(f32[1,64,64]{2,1,0:T(8,128)S(1)} %fusion.11), custom_call_target="InvertDiagBlocksLowerTriangular" | custom-call | tf_op jit(solution)/shard_map/triangular_solve | solution.py:55
  223.0 0.2 convolution_bitcast_fusion
  223.1 0.2 fusion.12
  223.3 0.0 copy-start.1
  223.3 0.2 subtract_multiply_fusion
  223.5 0.1 slice.30
  223.6 0.3 copy-done.1
  223.8 1.2 fusion.5
  225.0 1.3 fusion.18
  (8 shorter events, 0.1 us)
Async XLA Ops:
  7.2 41.3 %copy-start = (f32[65,8,512]{2,1,0:T(8,128)S(1)}, f32[65,8,512]{2,1,0:T(8,128)}, u32[]{:S(2)}) copy-start(f32[65,8,512]{2,1,0:T(8,128)} %param.4) | copy-start | bytes 3194884
  7.2 3.2 %copy-start.2 = (s32[512]{0:T(512)S(1)}, s32[512]{0:T(512)}, u32[]{:S(2)}) copy-start(s32[512]{0:T(512)} %param.6) | copy-start | bytes 6148
  7.2 3.2 %copy-start.3 = (s32[32]{0:T(128)S(1)}, s32[32]{0:T(128)}, u32[]{:S(2)}) copy-start(s32[32]{0:T(128)} %param.7) | copy-start | bytes 388
  7.2 40.3 %all-reduce.5.cloned.1.call-start = ((), (), s32[]{:S(2)}) async-start(), calls=%async_computation | async-start | bytes 294912 | tf_op jit(solution)/shard_map/psum | solution.py:16
  10.3 95.8 %all-reduce.7.cloned.1.call-start = ((), (), s32[]{:S(2)}) async-start(), calls=%async_computation.1 | async-start | bytes 294912 | tf_op jit(solution)/shard_map/psum | solution.py:16
  72.5 92.6 %all-reduce.9.cloned.1.call-start = ((), (), s32[]{:S(2)}) async-start(), calls=%async_computation.2 | async-start | bytes 294912 | tf_op jit(solution)/shard_map/psum | solution.py:16
  223.3 0.5 copy-start.1
Sparse Core Ops, SparseCore 0:
  10.4 37.0 all-reduce.4
  72.6 33.4 all-reduce.6
  131.6 33.4 all-reduce.8
where the time goes:
time: 233 us
  waiting for transfers between devices  104 us (45%)
  blocking collectives  87 us (37%)
  other arithmetic  23.1 us (10%)
  between operations  13.9 us (6%)
  matrix products  3.87 us (2%)
    psum x3, waiting for transfers between devices, firm_totals(): return lax.psum(jnp.sum(current, axis=1), 'day')  104 us
    psum x2, blocking collectives, axis_day_sum(): return lax.psum(day_part, 'firm')  45.3 us
    psum x1, blocking collectives, axis_day_gram(): return lax.psum((day_part, gram_part), 'firm')  23.2 us
    psum x1, blocking collectives, on_device(): gram = lax.psum(local_gram, 'day')  18.5 us
    another operation x3, other arithmetic, on_device(): factor = jnp.linalg.cholesky(matrix)  6.52 us
    another operation x2, other arithmetic, on_device(): lax.linalg.triangular_solve(factor, middle, left_side=True, lower=True, t...  5.55 us
  transfers between devices with their start and end apart: 3, of which 3 were waited for; matrix products, arithmetic and copies ran while one was open for 0% of the time, Pallas kernels for 0%

commit v1 on v0

v1 whole, which is shorter than its diff:
```python
import functools

import jax
import jax.numpy as jnp
from jax import lax
from jax.experimental import pallas as pl
from jax.experimental.pallas import tpu as pltpu
from jax.sharding import PartitionSpec as P

SWEEPS = 3
HIGHEST = lax.Precision.HIGHEST
MESH = pl.DeviceIdType.MESH


def up(n, m):
    return -(-n // m) * m


def nt(a, b):
    return lax.dot_general(
        a, b, (((1,), (1,)), ((), ())), precision=HIGHEST, preferred_element_type=jnp.float32
    )


def nn(a, b):
    return jnp.dot(a, b, precision=HIGHEST, preferred_element_type=jnp.float32)


def kernel(
    nf, nd, panel, presence, coef_ref, resid_ref,
    big, means, means_all, masks, alphas, alphas_in, part, part_in, mid, mid_in, full, vfull,
    s_a, r_a, s_m, r_m, s_1, r_1, s_2, r_2, s_3, r_3,
):
    cols, day_dev, firm_dev = panel.shape
    regs = cols - 1
    days = presence.shape[0]
    chunk = firm_dev // nd
    crow = up(cols, 8)
    width = full.shape[2]
    f = lax.axis_index("firm")
    d = lax.axis_index("day")

    def firm_peer(o):
        return lax.rem(f + o, nf)

    def day_peer(o):
        return lax.rem(d + o, nd)

    barrier = pltpu.get_barrier_semaphore()
    for o in range(1, nf):
        pl.semaphore_signal(barrier, inc=1, device_id=(firm_peer(o), d), device_id_type=MESH)
    for o in range(1, nd):
        pl.semaphore_signal(barrier, inc=1, device_id=(f, day_peer(o)), device_id_type=MESH)

    def send_day(o, src, dst, ssem, rsem):
        return pltpu.make_async_remote_copy(
            src_ref=src, dst_ref=dst, send_sem=ssem.at[o], recv_sem=rsem,
            device_id=(f, day_peer(o)), device_id_type=MESH)

    def send_firm(o, src, dst, ssem, rsem):
        return pltpu.make_async_remote_copy(
            src_ref=src, dst_ref=dst, send_sem=ssem.at[o], recv_sem=rsem,
            device_id=(firm_peer(o), d), device_id_type=MESH)

    mask = presence[...].astype(jnp.float32)
    for j in range(nd):
        masks[j] = mask[:, j * chunk:(j + 1) * chunk]
    here = presence[pl.ds(pl.multiple_of(d * day_dev, 8), day_dev), :].astype(jnp.float32)
    here_n = jnp.maximum(jnp.sum(here, axis=0, keepdims=True), 1.0)
    total = jnp.zeros((cols, firm_dev), jnp.float32)
    for t in range(day_dev):
        total = total + panel[:, t, :] * here[t:t + 1, :]
    alpha = total / here_n
    alphas[:, cols:, :] = jnp.zeros((nd, crow - cols, chunk), jnp.float32)
    for j in range(nd):
        alphas[j, :cols, :] = alpha[:, j * chunk:(j + 1) * chunk]
    pl.semaphore_wait(barrier, nf + nd - 2)
    sends = []
    for o in range(1, nd):
        c = send_day(o, alphas.at[day_peer(o)], alphas_in.at[d], s_a, r_a.at[d])
        c.start()
        sends.append(c)
    alphas_in[d] = alphas[d]

    big[cols:crow, :] = jnp.zeros((crow - cols, day_dev * firm_dev), jnp.float32)
    row_id = lax.broadcasted_iota(jnp.int32, (days, firm_dev), 0)
    for t in range(day_dev):
        lanes = slice(t * firm_dev, (t + 1) * firm_dev)
        big[:cols, lanes] = here[t:t + 1, :] * (panel[:, t, :] - alpha)
        big[crow:crow + days, lanes] = (row_id == d * day_dev + t).astype(jnp.float32)
    gram = nt(big[:crow, :], big[...])

    for o in range(1, nd):
        src = day_peer(o)
        send_day(o, alphas.at[src], alphas_in.at[src], s_a, r_a.at[src]).wait_recv()
    own = masks[d]
    counts = [
        jnp.sum(own[j * day_dev:(j + 1) * day_dev, :], axis=0, keepdims=True) for j in range(nd)
    ]
    n = functools.reduce(jnp.add, counts)
    blocks = [alphas_in[j] for j in range(nd)]
    mean = functools.reduce(jnp.add, [b * w for b, w in zip(blocks, counts)]) / n
    means_all[d] = mean
    for o in range(1, nd):
        c = send_day(o, means_all.at[d], means_all.at[d], s_m, r_m.at[d])
        c.start()
        sends.append(c)
    day_id = lax.broadcasted_iota(jnp.int32, (days, chunk), 0)
    for j in range(nd):
        delta = blocks[j] - mean
        lo = j * day_dev
        dummy = jnp.where((day_id >= lo) & (day_id < lo + day_dev), own, 0.0)
        gram = gram + nt(delta, jnp.concatenate([delta * counts[j], dummy], axis=0))
    share = nt(own, jnp.concatenate([jnp.zeros((crow, chunk), jnp.float32), own / n], axis=0))

    size = crow + days
    piece = part.shape[1]
    table = jnp.concatenate([gram, share], axis=0)
    if nf * piece > size:
        table = jnp.concatenate([table, jnp.zeros((nf * piece - size, size), jnp.float32)], axis=0)
    if width > size:
        table = jnp.concatenate([table, jnp.zeros((nf * piece, width - size), jnp.float32)], axis=1)
    part[...] = table.reshape(nf, piece, width)
    for o in range(1, nf):
        c = send_firm(o, part.at[firm_peer(o)], part_in.at[f], s_1, r_1.at[f])
        c.start()
        sends.append(c)
    part_in[f] = part[f]
    for o in range(1, nf):
        src = firm_peer(o)
        send_firm(o, part.at[src], part_in.at[src], s_1, r_1.at[src]).wait_recv()
    mid[d] = functools.reduce(jnp.add, [part_in[j] for j in range(nf)])
    for o in range(1, nd):
        c = send_day(o, mid.at[d], mid.at[d], s_2, r_2.at[d])
        c.start()
        sends.append(c)
    for o in range(1, nd):
        src = day_peer(o)
        send_day(o, mid.at[src], mid.at[src], s_2, r_2.at[src]).wait_recv()
    full[f] = functools.reduce(jnp.add, [mid[j] for j in range(nd)])
    for o in range(1, nf):
        c = send_firm(o, full.at[f], full.at[f], s_3, r_3.at[f])
        c.start()
        sends.append(c)
    for o in range(1, nf):
        src = firm_peer(o)
        send_firm(o, full.at[src], full.at[src], s_3, r_3.at[src]).wait_recv()

    table = full[...].reshape(nf * piece, width)
    gram = table[:crow, :crow]
    csum = table[:crow, crow:size]
    share = table[crow:size, crow:size]
    day_n = jnp.floor(jnp.sum(share, axis=0, keepdims=True) + 0.5)
    before = csum / day_n
    after = before
    for _ in range(SWEEPS - 1):
        before, after = after, (csum + nn(after, share)) / day_n
    step = after - before
    excess = step * day_n
    gram = gram - nt(csum, before) - nt(before, excess) - nt(excess, step)

    for o in range(1, nd):
        src = day_peer(o)
        send_day(o, means_all.at[src], means_all.at[src], s_m, r_m.at[src]).wait_recv()
    for j in range(nd):
        means[:, j * chunk:(j + 1) * chunk] = means_all[j]
    n_all = jnp.sum(mask, axis=0, keepdims=True)
    firm_eff = means[...] - nn(before, mask) / n_all
    after_t = after.T
    full_days = after_t[:days, :]

    aug = gram[:regs, :]
    rid = lax.broadcasted_iota(jnp.int32, aug.shape, 0)
    lid = lax.broadcasted_iota(jnp.int32, aug.shape, 1)
    for k in range(regs):
        row = aug[k:k + 1, :] / aug[k:k + 1, k:k + 1]
        col = jnp.where(rid[:, :1] == k, 0.0, aug[:, k:k + 1])
        aug = aug - col * row
    diag = jnp.sum(jnp.where(rid == lid, aug, 0.0), axis=1, keepdims=True)
    coef = aug[:, regs:regs + 1] / diag
    sq = (regs, regs)
    eye = lax.broadcasted_iota(jnp.int32, sq, 0) == lax.broadcasted_iota(jnp.int32, sq, 1)
    coef_ref[...] = jnp.sum(jnp.where(eye, coef, 0.0), axis=0, keepdims=True)

    vfull[...] = jnp.zeros(vfull.shape, jnp.float32)
    vfull[:regs, :] = jnp.broadcast_to(-coef, (regs, vfull.shape[1]))
    vfull[regs:cols, :] = jnp.ones((1, vfull.shape[1]), jnp.float32)
    v = vfull[:, :1]
    firm_part = jnp.sum(firm_eff * v, axis=0, keepdims=True)
    day_part = jnp.sum(after * v, axis=0, keepdims=True)
    day_sel = (lax.broadcasted_iota(jnp.int32, (day_dev, days), 1)
               == lax.broadcasted_iota(jnp.int32, (day_dev, days), 0) + d * day_dev)
    day_here = jnp.sum(jnp.where(day_sel, day_part, 0.0), axis=1, keepdims=True)
    acc = jnp.zeros((day_dev, firm_dev), jnp.float32)
    for c in range(cols):
        acc = acc + panel[c] * vfull[c:c + 1, :1]
    resid_ref[...] = here * (acc - firm_part - day_here)

    for c in sends:
        c.wait_send()


def on_device(nf, nd, panel, presence, firm_count, day_count):
    cols, day_dev, firm_dev = panel.shape
    days = presence.shape[0]
    chunk = firm_dev // nd
    crow = up(cols, 8)
    size = crow + days
    piece = up(-(-size // nf), 8)
    width = up(size, 128)
    vm = pl.BlockSpec(memory_space=pltpu.VMEM)
    f32 = jnp.float32
    dma = pltpu.SemaphoreType.DMA
    coef, resid = pl.pallas_call(
        functools.partial(kernel, nf, nd),
        out_shape=(jax.ShapeDtypeStruct((1, cols - 1), f32),
                   jax.ShapeDtypeStruct((day_dev, firm_dev), f32)),
        in_specs=[vm, vm],
        out_specs=(vm, vm),
        scratch_shapes=[
            pltpu.VMEM((size, day_dev * firm_dev), f32),
            pltpu.VMEM((crow, firm_dev), f32),
            pltpu.VMEM((nd, crow, chunk), f32),
            pltpu.VMEM((nd, days, chunk), f32),
            pltpu.VMEM((nd, crow, chunk), f32),
            pltpu.VMEM((nd, crow, chunk), f32),
            pltpu.VMEM((nf, piece, width), f32),
            pltpu.VMEM((nf, piece, width), f32),
            pltpu.VMEM((nd, piece, width), f32),
            pltpu.VMEM((8, 128), f32),
            pltpu.VMEM((nf, piece, width), f32),
            pltpu.VMEM((crow, 128), f32),
            dma((nd,)), dma((nd,)), dma((nd,)), dma((nd,)),
            dma((nf,)), dma((nf,)), dma((nd,)), dma((nd,)), dma((nf,)), dma((nf,)),
        ],
        compiler_params=pltpu.CompilerParams(
            collective_id=0, has_side_effects=True, vmem_limit_bytes=40 * 2**20
        ),
    )(panel, presence)
    return coef.reshape(cols - 1), resid


def solution(mesh):
    placed = (P(None, "day", "firm"), P(None, "firm"), P("firm"), P())
    body = functools.partial(on_device, mesh.shape["firm"], mesh.shape["day"])
    return jax.shard_map(
        body, mesh=mesh, in_specs=placed, out_specs=(P(), P("day", "firm")), check_vma=False
    )
```

time: 233 us -> 33.9 us (0.15)
  waiting for transfers between devices: 104 us -> 0 us
  blocking collectives: 87 us -> 0 us
  Pallas kernels: 0 us -> 29.9 us
  other arithmetic: 23.1 us -> 0 us
  between operations: 13.9 us -> 0.65 us
  matrix products: 3.87 us -> 0 us
  local copies, waits for them, and re-layouts: 0.51 us -> 3.18 us
    psum x3 -> x0, waiting for transfers between devices: 104 us -> none  [firm_totals(): return lax.psum(jnp.sum(current, axis=1), 'day')]
    psum x4 -> x0, blocking collectives: 87 us -> none  [the longest x2 45.3 us: axis_day_sum(): return lax.psum(day_part, 'firm')]
    pallas_call x0 -> x1, Pallas kernels: none -> 29.9 us  [on_device(): pl.pallas_call(functools.partial(kernel, nf, nd), out_shape=(jax.ShapeDty...]
    another operation x5 -> x0, other arithmetic: 12.1 us -> none  [the longest x3 6.52 us: on_device(): factor = jnp.linalg.cholesky(matrix)]
    reduce_sum x6 -> x0, other arithmetic: 5.94 us -> none  [the longest x3 4.65 us: firm_totals(): return lax.psum(jnp.sum(current, axis=1), 'day')]
    dot_general x3 -> x0, matrix products: 3.56 us -> none  [the longest x1 2.18 us: cross_products(): return jnp.dot(flat, flat.T, precision=lax.Precision.HIGHEST)]
    unnamed x8 -> x6, local copies, waits for them, and re-layouts: 0.29 us -> 3.18 us
    div x7 -> x0, other arithmetic: 2.82 us -> none  [the longest x3 2.78 us: on_device(): firm_mean = firm_totals(current) / firm_n]
  transfers between devices with their start and end apart: 3 -> 0, of which waited for: 3 -> 0; matrix products, arithmetic and copies ran while one was open for 0% -> 0% of each run, Pallas kernels for 0% -> 0%
where the time goes in v1:
time: 33.9 us; the launch traced here: 33.7 us
  Pallas kernels  29.9 us (88%)
  local copies, waits for them, and re-layouts  3.18 us (9%)
  between operations  0.65 us (2%)
    pallas_call x1, Pallas kernels, on_device(): pl.pallas_call(functools.partial(kernel, nf, nd), out_shape=(jax.ShapeDty...  29.9 us
    unnamed x6, local copies, waits for them, and re-layouts  3.18 us

profile of v1, /device:TPU:0, one launch (start us, length us, event | category | flops | bytes accessed | tf_op | source)
XLA Modules:
  0.0 33.7 jit_solution(643714481348068907)
XLA Ops:
  0.6 0.0 copy-start
  0.6 1.2 %copy-done = f32[65,8,512]{2,1,0:T(8,128)S(1)} copy-done((f32[65,8,512]{2,1,0:T(8,128)S(1)}, f32[65,8,512]{2,1,0:T(8,128)}, u32[]{:S(2)}) %copy-start) | copy-done | bytes 1064984
  1.9 0.0 copy-start.1
  1.9 0.8 %copy-done.1 = s32[32,512]{1,0:T(8,128)S(1)} copy-done((s32[32,512]{1,0:T(8,128)S(1)}, s32[32,512]{1,0:T(8,128)}, u32[]{:S(2)}) %copy-start.1) | copy-done | bytes 65560
  2.7 29.9 %shard_map.41 = (f32[1,64]{1,0:T(1,128)S(1)}, f32[8,512]{1,0:T(8,128)S(1)}) custom-call(f32[65,8,512]{2,1,0:T(8,128)S(1)} %copy-done, s32[32,512]{1,0:T(8,128)S(1)} %copy-done.1), custom_call_target="tpu_custom_call" | custom-call | tf_op jit(solution)/shard_map/pallas_call | solution.py:214
  32.6 0.5 %copy.6 = f32[64]{0:T(128)} copy(f32[64]{0:T(128)S(1)} %bitcast.1) | data formatting | bytes 512
  33.1 0.6 %copy.7 = f32[8,512]{1,0:T(8,128)} copy(f32[8,512]{1,0:T(8,128)S(1)} %get-tuple-element.9) | data formatting | bytes 32768
Async XLA Ops:
  0.6 1.2 %copy-start = (f32[65,8,512]{2,1,0:T(8,128)S(1)}, f32[65,8,512]{2,1,0:T(8,128)}, u32[]{:S(2)}) copy-start(f32[65,8,512]{2,1,0:T(8,128)} %panel.1) | copy-start | bytes 3194884
  1.9 0.8 %copy-start.1 = (s32[32,512]{1,0:T(8,128)S(1)}, s32[32,512]{1,0:T(8,128)}, u32[]{:S(2)}) copy-start(s32[32,512]{1,0:T(8,128)} %presence.1) | copy-start | bytes 196612

commit v2 on v1

v2 whole, which is shorter than its diff:
```python
import functools

import jax
import jax.numpy as jnp
from jax import lax
from jax.experimental import pallas as pl
from jax.experimental.pallas import tpu as pltpu
from jax.sharding import PartitionSpec as P

SWEEPS = 3
HIGHEST = lax.Precision.HIGHEST
MESH = pl.DeviceIdType.MESH


def up(n, m):
    return -(-n // m) * m


def nt(a, b):
    return lax.dot_general(
        a, b, (((1,), (1,)), ((), ())), precision=HIGHEST, preferred_element_type=jnp.float32
    )


def nn(a, b):
    return jnp.dot(a, b, precision=HIGHEST, preferred_element_type=jnp.float32)


def split(x):
    hi = x.astype(jnp.bfloat16)
    return hi, (x - hi.astype(jnp.float32)).astype(jnp.bfloat16)


def nt16(a, b):
    return lax.dot_general(a, b, (((1,), (1,)), ((), ())), preferred_element_type=jnp.float32)


def inverse2(p):
    (a, b), (c, e) = p
    r = 1.0 / (a * e - b * c)
    return [[e * r, -b * r], [-c * r, a * r]]


def times(p, rows):
    return [p[0][0] * rows[0] + p[0][1] * rows[1], p[1][0] * rows[0] + p[1][1] * rows[1]]


def solve4(p, rows):
    top = inverse2([p[0][:2], p[1][:2]])
    right = [[p[0][2], p[0][3]], [p[1][2], p[1][3]]]
    low = [p[2][:2], p[3][:2]]
    cols = [times(top, [right[0][j], right[1][j]]) for j in range(2)]
    schur = [[None, None], [None, None]]
    for j in range(2):
        down = times(low, cols[j])
        for i in range(2):
            schur[i][j] = p[2 + i][2 + j] - down[i]
    bottom = inverse2(schur)
    up_rows = times(top, rows[:2])
    down = times(low, up_rows)
    under = times(bottom, [rows[2] - down[0], rows[3] - down[1]])
    return [
        up_rows[0] - cols[0][0] * under[0] - cols[1][0] * under[1],
        up_rows[1] - cols[0][1] * under[0] - cols[1][1] * under[1],
    ] + under


def eliminate(mat, regs):
    tiles = [mat[8 * i:8 * i + 8, :] for i in range(regs // 8)]
    shape = tiles[0].shape
    sub = lax.broadcasted_iota(jnp.int32, shape, 0)
    for k in range(0, regs, 4):
        at, lo = k // 8, k % 8
        col = [[jnp.broadcast_to(t[:, k + j:k + j + 1], shape) for t in tiles] for j in range(4)]
        p = [[col[j][at][lo + i:lo + i + 1, :] for j in range(4)] for i in range(4)]
        rows = solve4(p, [tiles[at][lo + i:lo + i + 1, :] for i in range(4)])
        out = []
        for i, t in enumerate(tiles):
            t = t - (col[0][i] * rows[0] + col[1][i] * rows[1]) - (col[2][i] * rows[2] + col[3][i] * rows[3])
            if i == at:
                for j in range(4):
                    t = jnp.where(sub == lo + j, rows[j], t)
            out.append(t)
        tiles = out
    return tiles


def kernel(
    nf, nd, panel_hbm, presence_hbm, coef_ref, resid_ref,
    panel, presence, big, left, right, means, means_all, masks, alphas, alphas_in,
    part, part_in, mid, full, vfull,
    s_in, s_a, r_a, s_m, r_m, s_1, r_1, s_2, r_2, s_3, r_3,
):
    cols, day_dev, firm_dev = panel_hbm.shape
    regs = cols - 1
    days = presence.shape[0]
    chunk = firm_dev // nd
    crow = up(cols, 8)
    xrow = panel.shape[0]
    half = right.shape[0] // 2
    piece, width = part.shape[1:]
    f = lax.axis_index("firm")
    d = lax.axis_index("day")
    f32 = jnp.float32

    def firm_peer(o):
        return lax.rem(f + o, nf)

    def day_peer(o):
        return lax.rem(d + o, nd)

    load_mask = pltpu.make_async_copy(presence_hbm, presence, s_in.at[0])
    load_mask.start()
    load_panel = pltpu.make_async_copy(panel_hbm, panel.at[pl.ds(0, cols)], s_in.at[1])
    load_panel.start()
    barrier = pltpu.get_barrier_semaphore()
    for o in range(1, nf):
        pl.semaphore_signal(barrier, inc=1, device_id=(firm_peer(o), d), device_id_type=MESH)
    for o in range(1, nd):
        pl.semaphore_signal(barrier, inc=1, device_id=(f, day_peer(o)), device_id_type=MESH)

    def send_day(o, src, dst, ssem, rsem):
        return pltpu.make_async_remote_copy(
            src_ref=src, dst_ref=dst, send_sem=ssem.at[o], recv_sem=rsem,
            device_id=(f, day_peer(o)), device_id_type=MESH)

    def send_firm(o, src, dst, ssem, rsem):
        return pltpu.make_async_remote_copy(
            src_ref=src, dst_ref=dst, send_sem=ssem.at[o], recv_sem=rsem,
            device_id=(firm_peer(o), d), device_id_type=MESH)

    panel[cols:, :, :] = jnp.zeros((xrow - cols, day_dev, firm_dev), f32)
    row_id = lax.broadcasted_iota(jnp.int32, (half - xrow, firm_dev), 0)
    for t in range(day_dev):
        lanes = slice(t * firm_dev, (t + 1) * firm_dev)
        big[xrow:half, lanes] = (row_id == d * day_dev + t).astype(f32).astype(jnp.bfloat16)
    if half > xrow:
        big[half + xrow:, :] = jnp.zeros((half - xrow, day_dev * firm_dev), jnp.bfloat16)
    load_mask.wait()
    mask = presence[...].astype(f32)
    for j in range(nd):
        masks[j] = mask[:, j * chunk:(j + 1) * chunk]
    here = presence[pl.ds(pl.multiple_of(d * day_dev, 8), day_dev), :].astype(f32)
    here_n = jnp.maximum(jnp.sum(here, axis=0, keepdims=True), 1.0)
    own = masks[d]
    counts = [
        jnp.sum(own[j * day_dev:(j + 1) * day_dev, :], axis=0, keepdims=True) for j in range(nd)
    ]
    n = functools.reduce(jnp.add, counts)
    day_id = lax.broadcasted_iota(jnp.int32, (days, chunk), 0)
    share = split(own / n)
    fill = jnp.zeros((xrow - crow, chunk), f32)
    tail = [jnp.zeros((half - xrow - days, chunk), f32)] if half > xrow + days else []

    load_panel.wait()
    total = panel[:crow, 0, :] * here[0:1, :]
    for t in range(1, day_dev):
        total = total + panel[:crow, t, :] * here[t:t + 1, :]
    alpha = total / here_n
    for j in range(nd):
        alphas[j] = alpha[:, j * chunk:(j + 1) * chunk]
    pl.semaphore_wait(barrier, nf + nd - 2)
    sends = []
    for o in range(1, nd):
        c = send_day(o, alphas.at[day_peer(o)], alphas_in.at[d], s_a, r_a.at[d])
        c.start()
        sends.append(c)
    alphas_in[d] = alphas[d]

    base = jnp.concatenate([alpha, jnp.zeros((xrow - crow, firm_dev), f32)], axis=0)
    for t in range(day_dev):
        lanes = slice(t * firm_dev, (t + 1) * firm_dev)
        hi, lo = split(here[t:t + 1, :] * (panel[:, t, :] - base))
        big[:xrow, lanes] = hi
        big[half:half + xrow, lanes] = lo
    inner = nt16(jnp.concatenate([big[:xrow, :], big[half:half + xrow, :]], axis=0), big[...])

    for o in range(1, nd):
        src = day_peer(o)
        send_day(o, alphas.at[src], alphas_in.at[src], s_a, r_a.at[src]).wait_recv()
    blocks = [alphas_in[j] for j in range(nd)]
    mean = functools.reduce(jnp.add, [b * w for b, w in zip(blocks, counts)]) / n
    means_all[d] = mean
    for j in range(nd):
        lanes = slice(j * chunk, (j + 1) * chunk)
        delta = jnp.concatenate([blocks[j] - mean, fill], axis=0)
        first = j * day_dev
        dummy = jnp.where((day_id >= first) & (day_id < first + day_dev), own, 0.0)
        hi, lo = split(delta)
        left[:xrow, lanes] = hi
        left[xrow:2 * xrow, lanes] = lo
        left[2 * xrow:2 * xrow + days, lanes] = share[0]
        left[2 * xrow + days:, lanes] = share[1]
        hi, lo = split(jnp.concatenate([delta * counts[j], dummy] + tail, axis=0))
        right[:half, lanes] = hi
        right[half:, lanes] = lo
    outer = nt16(left[...], right[...])
    both = inner + outer[:2 * xrow, :]
    both = both[:, :half] + both[:, half:]
    table = jnp.concatenate(
        [both[:xrow, :] + both[xrow:, :],
         outer[2 * xrow:2 * xrow + days, :half] + outer[2 * xrow + days:, :half]], axis=0
    )

    if nf * piece > xrow + days:
        table = jnp.concatenate([table, jnp.zeros((nf * piece - xrow - days, width), f32)], axis=0)
    part[...] = table.reshape(nf, piece, width)
    for o in range(1, nf):
        c = send_firm(o, part.at[firm_peer(o)], part_in.at[f], s_1, r_1.at[f])
        c.start()
        sends.append(c)
    part_in[f] = part[f]
    for o in range(1, nf):
        src = firm_peer(o)
        send_firm(o, part.at[src], part_in.at[src], s_1, r_1.at[src]).wait_recv()
    mid[d] = functools.reduce(jnp.add, [part_in[j] for j in range(nf)])
    for o in range(1, nd):
        c = send_day(o, mid.at[d], mid.at[d], s_2, r_2.at[d])
        c.start()
        sends.append(c)
    for o in range(1, nd):
        c = send_day(o, means_all.at[d], means_all.at[d], s_m, r_m.at[d])
        c.start()
        sends.append(c)
    for o in range(1, nd):
        src = day_peer(o)
        send_day(o, mid.at[src], mid.at[src], s_2, r_2.at[src]).wait_recv()
    full[f] = functools.reduce(jnp.add, [mid[j] for j in range(nd)])
    for o in range(1, nf):
        c = send_firm(o, full.at[f], full.at[f], s_3, r_3.at[f])
        c.start()
        sends.append(c)
    for o in range(1, nf):
        src = firm_peer(o)
        send_firm(o, full.at[src], full.at[src], s_3, r_3.at[src]).wait_recv()

    table = full[...].reshape(nf * piece, width)
    csum = table[:xrow, xrow:xrow + days]
    cross = table[xrow:xrow + days, xrow:xrow + days]
    day_n = jnp.floor(jnp.sum(cross, axis=0, keepdims=True) + 0.5)
    before = csum / day_n
    after = before
    for _ in range(SWEEPS - 1):
        before, after = after, (csum + nn(after, cross)) / day_n
    step = after - before
    excess = step * day_n
    gram = table[:regs, :xrow] - (
        nt(csum[:regs], before) + nt(before[:regs], excess) + nt(excess[:regs], step)
    )

    tiles = eliminate(gram, regs)
    shape = (8, vfull.shape[1])
    sub = lax.broadcasted_iota(jnp.int32, shape, 0)
    lane = lax.broadcasted_iota(jnp.int32, shape, 1)
    picked = jnp.zeros(shape, f32)
    for i, t in enumerate(tiles):
        value = jnp.broadcast_to(t[:, regs:regs + 1], shape)
        vfull[8 * i:8 * i + 8, :] = -value
        picked = picked + jnp.where(lane == sub + 8 * i, value, 0.0)
    coef_ref[...] = jnp.sum(picked, axis=0, keepdims=True)[:, :regs]
    vfull[regs:, :] = jnp.where(
        lax.broadcasted_iota(jnp.int32, (xrow - regs, vfull.shape[1]), 0) == 0, 1.0, 0.0
    )

    acc = panel[0] * vfull[0:1, :1]
    for c in range(1, cols):
        acc = acc + panel[c] * vfull[c:c + 1, :1]
    v = vfull[:, :1]
    hi, lo = split(jnp.broadcast_to(jnp.sum(before * v, axis=0, keepdims=True), (8, days)))
    lead = jnp.concatenate([hi, lo], axis=0)
    spread = jnp.dot(lead, mask.astype(jnp.bfloat16), preferred_element_type=f32)
    spread = spread[0:1, :] + spread[8:9, :]
    day_part = jnp.sum(after * v, axis=0, keepdims=True)
    day_sel = (lax.broadcasted_iota(jnp.int32, (day_dev, days), 1)
               == lax.broadcasted_iota(jnp.int32, (day_dev, days), 0) + d * day_dev)
    day_here = jnp.sum(jnp.where(day_sel, day_part, 0.0), axis=1, keepdims=True)
    for o in range(1, nd):
        src = day_peer(o)
        send_day(o, means_all.at[src], means_all.at[src], s_m, r_m.at[src]).wait_recv()
    for j in range(nd):
        means[:, j * chunk:(j + 1) * chunk] = means_all[j]
    n_all = jnp.sum(mask, axis=0, keepdims=True)
    firm_part = jnp.sum(means[...] * vfull[:crow, :1], axis=0, keepdims=True) - spread / n_all
    resid_ref[...] = here * (acc - firm_part - day_here)

    for c in sends:
        c.wait_send()


def on_device(nf, nd, panel, presence, firm_count, day_count):
    cols, day_dev, firm_dev = panel.shape
    days = presence.shape[0]
    chunk = firm_dev // nd
    crow = up(cols, 8)
    xrow = up(cols, 16)
    half = up(xrow + days, 128)
    piece = up(-(-(xrow + days) // nf), 8)
    anywhere = pl.BlockSpec(memory_space=pl.ANY)
    vm = pl.BlockSpec(memory_space=pltpu.VMEM)
    f32 = jnp.float32
    b16 = jnp.bfloat16
    dma = pltpu.SemaphoreType.DMA
    coef, resid = pl.pallas_call(
        functools.partial(kernel, nf, nd),
        out_shape=(jax.ShapeDtypeStruct((1, cols - 1), f32),
                   jax.ShapeDtypeStruct((day_dev, firm_dev), f32)),
        in_specs=[anywhere, anywhere],
        out_specs=(vm, vm),
        scratch_shapes=[
            pltpu.VMEM((xrow, day_dev, firm_dev), f32),
            pltpu.VMEM((days, firm_dev), jnp.int32),
            pltpu.VMEM((2 * half, day_dev * firm_dev), b16),
            pltpu.VMEM((2 * (xrow + days), firm_dev), b16),
            pltpu.VMEM((2 * half, firm_dev), b16),
            pltpu.VMEM((crow, firm_dev), f32),
            pltpu.VMEM((nd, crow, chunk), f32),
            pltpu.VMEM((nd, days, chunk), f32),
            pltpu.VMEM((nd, crow, chunk), f32),
            pltpu.VMEM((nd, crow, chunk), f32),
            pltpu.VMEM((nf, piece, half), f32),
            pltpu.VMEM((nf, piece, half), f32),
            pltpu.VMEM((nd, piece, half), f32),
            pltpu.VMEM((nf, piece, half), f32),
            pltpu.VMEM((xrow, 128), f32),
            dma((2,)), dma((nd,)), dma((nd,)), dma((nd,)), dma((nd,)),
            dma((nf,)), dma((nf,)), dma((nd,)), dma((nd,)), dma((nf,)), dma((nf,)),
        ],
        compiler_params=pltpu.CompilerParams(collective_id=0, has_side_effects=True),
    )(panel, presence)
    return coef.reshape(cols - 1), resid


def solution(mesh):
    placed = (P(None, "day", "firm"), P(None, "firm"), P("firm"), P())
    body = functools.partial(on_device, mesh.shape["firm"], mesh.shape["day"])
    return jax.shard_map(
        body, mesh=mesh, in_specs=placed, out_specs=(P(), P("day", "firm")), check_vma=False
    )
```

time: 33.9 us -> 30 us (0.88)
  Pallas kernels: 29.9 us -> 26.6 us
  local copies, waits for them, and re-layouts: 3.18 us -> 2.46 us
    pallas_call x1, Pallas kernels: 29.9 us -> 26.6 us  [on_device(): pl.pallas_call(functools.partial(kernel, nf, nd), out_shape=(jax.ShapeDty...]
    unnamed x6 -> x2, local copies, waits for them, and re-layouts: 3.18 us -> 2.46 us
where the time goes in v2:
time: 30 us; the launch traced here: 29.7 us
  Pallas kernels  26.6 us (89%)
  local copies, waits for them, and re-layouts  2.46 us (8%)
  between operations  0.64 us (2%)
    pallas_call x1, Pallas kernels, on_device(): pl.pallas_call(functools.partial(kernel, nf, nd), out_shape=(jax.ShapeDty...  26.6 us
    unnamed x2, local copies, waits for them, and re-layouts  2.46 us

profile of v2, /device:TPU:0, one launch (start us, length us, event | category | flops | bytes accessed | tf_op | source)
XLA Modules:
  0.0 29.7 jit_solution(1044867019329964047)
XLA Ops:
  0.6 26.6 %shard_map.41 = (f32[1,64]{1,0:T(1,128)}, f32[8,512]{1,0:T(8,128)}) custom-call(f32[65,8,512]{2,1,0:T(8,128)} %panel_hbm.1, s32[32,512]{1,0:T(8,128)} %presence_hbm.1), custom_call_target="tpu_custom_call" | custom-call | tf_op jit(solution)/shard_map/pallas_call | solution.py:303
  27.3 1.1 %copy.6 = f32[64]{0:T(128)} copy(f32[64]{0:T(128)} %bitcast.1) | data formatting | bytes 512
  28.4 1.3 %copy.7 = f32[8,512]{1,0:T(8,128)} copy(f32[8,512]{1,0:T(8,128)} %get-tuple-element.9) | data formatting | bytes 32768

commit v3 on v2

--- a/solution.py
+++ b/solution.py
@@ -91,12 +91,14 @@
     part, part_in, mid, full, vfull,
     s_in, s_a, r_a, s_m, r_m, s_1, r_1, s_2, r_2, s_3, r_3,
 ):
-    cols, day_dev, firm_dev = panel_hbm.shape
+    day_dev, firm_dev = resid_ref.shape
+    cols = panel_hbm.shape[0] // day_dev
     regs = cols - 1
     days = presence.shape[0]
     chunk = firm_dev // nd
     crow = up(cols, 8)
-    xrow = panel.shape[0]
+    xrow = panel.shape[1] // day_dev
+    tiles128 = range(firm_dev // 128)
     half = right.shape[0] // 2
     piece, width = part.shape[1:]
     f = lax.axis_index("firm")
@@ -111,8 +113,13 @@
 
     load_mask = pltpu.make_async_copy(presence_hbm, presence, s_in.at[0])
     load_mask.start()
-    load_panel = pltpu.make_async_copy(panel_hbm, panel.at[pl.ds(0, cols)], s_in.at[1])
-    load_panel.start()
+    load_panel = [
+        pltpu.make_async_copy(
+            panel_hbm.at[:, pl.ds(q * 128, 128)], panel.at[q, pl.ds(0, cols * day_dev)], s_in.at[1 + q])
+        for q in tiles128
+    ]
+    for c in load_panel:
+        c.start()
     barrier = pltpu.get_barrier_semaphore()
     for o in range(1, nf):
         pl.semaphore_signal(barrier, inc=1, device_id=(firm_peer(o), d), device_id_type=MESH)
@@ -129,7 +136,11 @@
             src_ref=src, dst_ref=dst, send_sem=ssem.at[o], recv_sem=rsem,
             device_id=(firm_peer(o), d), device_id_type=MESH)
 
-    panel[cols:, :, :] = jnp.zeros((xrow - cols, day_dev, firm_dev), f32)
+    panel[:, cols * day_dev:, :] = jnp.zeros((len(tiles128), (xrow - cols) * day_dev, 128), f32)
+
+    def on_day(q, t, rows):
+        return panel[q, pl.ds(t, rows, stride=day_dev), :]
+
     row_id = lax.broadcasted_iota(jnp.int32, (half - xrow, firm_dev), 0)
     for t in range(day_dev):
         lanes = slice(t * firm_dev, (t + 1) * firm_dev)
@@ -152,27 +163,35 @@
     fill = jnp.zeros((xrow - crow, chunk), f32)
     tail = [jnp.zeros((half - xrow - days, chunk), f32)] if half > xrow + days else []
 
-    load_panel.wait()
-    total = panel[:crow, 0, :] * here[0:1, :]
-    for t in range(1, day_dev):
-        total = total + panel[:crow, t, :] * here[t:t + 1, :]
-    alpha = total / here_n
-    for j in range(nd):
-        alphas[j] = alpha[:, j * chunk:(j + 1) * chunk]
     pl.semaphore_wait(barrier, nf + nd - 2)
     sends = []
-    for o in range(1, nd):
-        c = send_day(o, alphas.at[day_peer(o)], alphas_in.at[d], s_a, r_a.at[d])
-        c.start()
-        sends.append(c)
+    alpha = []
+    for q in tiles128:
+        lanes = slice(q * 128, q * 128 + 128)
+        load_panel[q].wait()
+        total = on_day(q, 0, crow) * here[0:1, lanes]
+        for t in range(1, day_dev):
+            total = total + on_day(q, t, crow) * here[t:t + 1, lanes]
+        alpha.append(total / here_n[:, lanes])
+        for j in range(q * 128 // chunk, (q + 1) * 128 // chunk):
+            first = j * chunk - q * 128
+            alphas[j] = alpha[q][:, first:first + chunk]
+
+            @pl.when(d != j)
+            def _(j=j):
+                pltpu.make_async_remote_copy(
+                    src_ref=alphas.at[j], dst_ref=alphas_in.at[d], send_sem=s_a.at[j],
+                    recv_sem=r_a.at[d], device_id=(f, j), device_id_type=MESH).start()
+
     alphas_in[d] = alphas[d]
 
-    base = jnp.concatenate([alpha, jnp.zeros((xrow - crow, firm_dev), f32)], axis=0)
-    for t in range(day_dev):
-        lanes = slice(t * firm_dev, (t + 1) * firm_dev)
-        hi, lo = split(here[t:t + 1, :] * (panel[:, t, :] - base))
-        big[:xrow, lanes] = hi
-        big[half:half + xrow, lanes] = lo
+    for q in tiles128:
+        base = jnp.concatenate([alpha[q], jnp.zeros((xrow - crow, 128), f32)], axis=0)
+        for t in range(day_dev):
+            lanes = slice(t * firm_dev + q * 128, t * firm_dev + q * 128 + 128)
+            hi, lo = split(here[t:t + 1, q * 128:q * 128 + 128] * (on_day(q, t, xrow) - base))
+            big[:xrow, lanes] = hi
+            big[half:half + xrow, lanes] = lo
     inner = nt16(jnp.concatenate([big[:xrow, :], big[half:half + xrow, :]], axis=0), big[...])
 
     for o in range(1, nd):
@@ -262,10 +281,12 @@
         lax.broadcasted_iota(jnp.int32, (xrow - regs, vfull.shape[1]), 0) == 0, 1.0, 0.0
     )
 
-    acc = panel[0] * vfull[0:1, :1]
-    for c in range(1, cols):
-        acc = acc + panel[c] * vfull[c:c + 1, :1]
-    v = vfull[:, :1]
+    acc = []
+    for q in tiles128:
+        terms = [panel[q, c * day_dev:(c + 1) * day_dev, :] * vfull[c:c + 1, :] for c in range(cols)]
+        acc.append(functools.reduce(jnp.add, terms))
+    acc = jnp.concatenate(acc, axis=1)
+    v = vfull[:, :days]
     hi, lo = split(jnp.broadcast_to(jnp.sum(before * v, axis=0, keepdims=True), (8, days)))
     lead = jnp.concatenate([hi, lo], axis=0)
     spread = jnp.dot(lead, mask.astype(jnp.bfloat16), preferred_element_type=f32)
@@ -280,9 +301,16 @@
     for j in range(nd):
         means[:, j * chunk:(j + 1) * chunk] = means_all[j]
     n_all = jnp.sum(mask, axis=0, keepdims=True)
-    firm_part = jnp.sum(means[...] * vfull[:crow, :1], axis=0, keepdims=True) - spread / n_all
+    firm_part = jnp.concatenate(
+        [jnp.sum(means[:, q:q + 128] * vfull[:crow, :], axis=0, keepdims=True)
+         for q in range(0, firm_dev, 128)], axis=1) - spread / n_all
     resid_ref[...] = here * (acc - firm_part - day_here)
 
+    for o in range(1, nd):
+        to = day_peer(o)
+        pltpu.make_async_remote_copy(
+            src_ref=alphas.at[to], dst_ref=alphas_in.at[d], send_sem=s_a.at[to],
+            recv_sem=r_a.at[d], device_id=(f, to), device_id_type=MESH).wait_send()
     for c in sends:
         c.wait_send()
 
@@ -295,7 +323,7 @@
     xrow = up(cols, 16)
     half = up(xrow + days, 128)
     piece = up(-(-(xrow + days) // nf), 8)
-    anywhere = pl.BlockSpec(memory_space=pl.ANY)
+    hbm = pl.BlockSpec(memory_space=pltpu.HBM)
     vm = pl.BlockSpec(memory_space=pltpu.VMEM)
     f32 = jnp.float32
     b16 = jnp.bfloat16
@@ -304,10 +332,10 @@
         functools.partial(kernel, nf, nd),
         out_shape=(jax.ShapeDtypeStruct((1, cols - 1), f32),
                    jax.ShapeDtypeStruct((day_dev, firm_dev), f32)),
-        in_specs=[anywhere, anywhere],
+        in_specs=[hbm, hbm],
         out_specs=(vm, vm),
         scratch_shapes=[
-            pltpu.VMEM((xrow, day_dev, firm_dev), f32),
+            pltpu.VMEM((firm_dev // 128, xrow * day_dev, 128), f32),
             pltpu.VMEM((days, firm_dev), jnp.int32),
             pltpu.VMEM((2 * half, day_dev * firm_dev), b16),
             pltpu.VMEM((2 * (xrow + days), firm_dev), b16),
@@ -322,11 +350,11 @@
             pltpu.VMEM((nd, piece, half), f32),
             pltpu.VMEM((nf, piece, half), f32),
             pltpu.VMEM((xrow, 128), f32),
-            dma((2,)), dma((nd,)), dma((nd,)), dma((nd,)), dma((nd,)),
+            dma((1 + firm_dev // 128,)), dma((nd,)), dma((nd,)), dma((nd,)), dma((nd,)),
             dma((nf,)), dma((nf,)), dma((nd,)), dma((nd,)), dma((nf,)), dma((nf,)),
         ],
         compiler_params=pltpu.CompilerParams(collective_id=0, has_side_effects=True),
-    )(panel, presence)
+    )(panel.reshape(cols * day_dev, firm_dev), presence)
     return coef.reshape(cols - 1), resid
 
 

time: 30 us -> 30.1 us (level)
  no operation moved by 1% of the time
where the time goes in v3:
time: 30.1 us; the launch traced here: 29.8 us
  Pallas kernels  26.7 us (89%)
  local copies, waits for them, and re-layouts  2.46 us (8%)
  between operations  0.64 us (2%)
    pallas_call x1, Pallas kernels, on_device(): pl.pallas_call(functools.partial(kernel, nf, nd), out_shape=(jax.ShapeDty...  26.7 us
    unnamed x2, local copies, waits for them, and re-layouts  2.46 us

profile of v3, /device:TPU:0, one launch (start us, length us, event | category | flops | bytes accessed | tf_op | source)
XLA Modules:
  0.0 29.8 jit_solution(2556765063194600438)
XLA Ops:
  0.6 26.7 %shard_map.41 = (f32[1,64]{1,0:T(1,128)}, f32[8,512]{1,0:T(8,128)}) custom-call(f32[520,512]{1,0:T(8,128)} %bitcast.2, s32[32,512]{1,0:T(8,128)} %presence_hbm.1), custom_call_target="tpu_custom_call" | custom-call | tf_op jit(solution)/shard_map/pallas_call | solution.py:331
  27.3 1.1 %copy.6 = f32[64]{0:T(128)} copy(f32[64]{0:T(128)} %bitcast.3) | data formatting | bytes 512
  28.5 1.3 %copy.7 = f32[8,512]{1,0:T(8,128)} copy(f32[8,512]{1,0:T(8,128)} %get-tuple-element.9) | data formatting | bytes 32768

commit v4 on v3

--- a/solution.py
+++ b/solution.py
@@ -8,22 +8,11 @@
 from jax.sharding import PartitionSpec as P
 
 SWEEPS = 3
-HIGHEST = lax.Precision.HIGHEST
 MESH = pl.DeviceIdType.MESH
 
 
 def up(n, m):
     return -(-n // m) * m
-
-
-def nt(a, b):
-    return lax.dot_general(
-        a, b, (((1,), (1,)), ((), ())), precision=HIGHEST, preferred_element_type=jnp.float32
-    )
-
-
-def nn(a, b):
-    return jnp.dot(a, b, precision=HIGHEST, preferred_element_type=jnp.float32)
 
 
 def split(x):
@@ -35,9 +24,17 @@
     return lax.dot_general(a, b, (((1,), (1,)), ((), ())), preferred_element_type=jnp.float32)
 
 
+def nt(a, b):
+    a, b = split(a), split(b)
+    return nt16(a[0], b[0]) + (nt16(a[0], b[1]) + nt16(a[1], b[0]))
+
+
 def inverse2(p):
     (a, b), (c, e) = p
-    r = 1.0 / (a * e - b * c)
+    det = a * e - b * c
+    r = pl.reciprocal(det, approx=True)
+    r = r * (2.0 - det * r)
+    r = r * (2.0 - det * r)
     return [[e * r, -b * r], [-c * r, a * r]]
 
 
@@ -260,7 +257,7 @@
     before = csum / day_n
     after = before
     for _ in range(SWEEPS - 1):
-        before, after = after, (csum + nn(after, cross)) / day_n
+        before, after = after, (csum + nt(after, cross)) / day_n
     step = after - before
     excess = step * day_n
     gram = table[:regs, :xrow] - (

time: 30.1 us -> 30.1 us (level)
  no operation moved by 1% of the time
where the time goes in v4:
time: 30.1 us; the launch traced here: 29.9 us
  Pallas kernels  26.8 us (89%)
  local copies, waits for them, and re-layouts  2.46 us (8%)
  between operations  0.64 us (2%)
    pallas_call x1, Pallas kernels, on_device(): pl.pallas_call(functools.partial(kernel, nf, nd), out_shape=(jax.ShapeDty...  26.8 us
    unnamed x2, local copies, waits for them, and re-layouts  2.46 us

profile of v4, /device:TPU:0, one launch (start us, length us, event | category | flops | bytes accessed | tf_op | source)
XLA Modules:
  0.0 29.9 jit_solution(16765447018256171765)
XLA Ops:
  0.6 26.8 %shard_map.41 = (f32[1,64]{1,0:T(1,128)}, f32[8,512]{1,0:T(8,128)}) custom-call(f32[520,512]{1,0:T(8,128)} %bitcast.2, s32[32,512]{1,0:T(8,128)} %presence_hbm.1), custom_call_target="tpu_custom_call" | custom-call | tf_op jit(solution)/shard_map/pallas_call | solution.py:328
  27.4 1.1 %copy.6 = f32[64]{0:T(128)} copy(f32[64]{0:T(128)} %bitcast.3) | data formatting | bytes 512
  28.6 1.3 %copy.7 = f32[8,512]{1,0:T(8,128)} copy(f32[8,512]{1,0:T(8,128)} %get-tuple-element.9) | data formatting | bytes 32768
